TPU v7x, 128 devices: a whole 4x4x4 slice. The times are simulated.
128 devices in a mesh: dp: 8 (over x_lo, y), ctx: 16 (over x_hi, z, core).
Axes of the slice: x: 4 (x_hi: 2, x_lo: 2; x = x_hi * 2 + x_lo), y: 4, z: 4, core: 2. Of those that a mesh axis runs over, the one named last changes fastest.
Arguments:
- query_rows: bfloat16 [8, 2048, 4096], P('dp', 'ctx'), may hold values from -6 to 6
- key_rows: bfloat16 [8, 2048, 4096], P('dp', 'ctx'), may hold values from -6 to 6
- value_rows: bfloat16 [8, 2048, 4096], P('dp', 'ctx'), may hold values from -6 to 6
- grad_out: bfloat16 [8, 2048, 4096], P('dp', 'ctx'), may hold values from -6 to 6
- filter_taps: float32 [2048, 4096], P(None, 'ctx'), may hold values from -1.1 to 1.1
- skip_gain: float32 [4096], P('ctx'), may hold values from -1.5 to 1.5
Outputs:
- grad_query: bfloat16 [8, 2048, 4096], P('dp', 'ctx')
- grad_key: bfloat16 [8, 2048, 4096], P('dp', 'ctx')
- grad_value: bfloat16 [8, 2048, 4096], P('dp', 'ctx')
- grad_filter: float32 [2048, 4096], P('dp', 'ctx')
- grad_skip: float32 [4096], P(('ctx', 'dp'))
All inputs are finite; a program needn't handle non-finite values.
Results may differ from a plain program's by a relative error of at most 0.013.
Values may be sent and summed in bfloat16 or wider, within the bound.
A program may use at most 192 MiB of HBM per device.

v0:
```python
import functools

import jax
import jax.numpy as jnp
from jax import lax
from jax.experimental import pallas as pl
from jax.experimental.pallas import tpu as pltpu
from jax.sharding import PartitionSpec as P

F32 = jnp.float32
BF16 = jnp.bfloat16
B = 128
LIMIT = 56 * 1024 * 1024


def dot_nn(a, b):
    return lax.dot_general(a, b, (((1,), (0,)), ((), ())), preferred_element_type=F32)


def dot_nt(a, b):
    return lax.dot_general(a, b, (((1,), (1,)), ((), ())), preferred_element_type=F32)


def iotas(shape):
    return (
        lax.broadcasted_iota(jnp.int32, shape, 0),
        lax.broadcasted_iota(jnp.int32, shape, 1),
    )


def one_hot(cond):
    return jnp.where(cond, 1.0, 0.0).astype(BF16)


def product(a, b):
    return (a.astype(F32) * b.astype(F32)).astype(BF16)


def prepare_kernel(share, q_ref, k_ref, v_ref, o_ref, s_ref):
    rows, cols = iotas((256, 256))
    eye = one_hot(rows == cols)
    for m in range(q_ref.shape[1] // 256):
        at = slice(256 * m, 256 * m + 256)
        per = 256 // share
        for which, (a, b) in enumerate(((k_ref, v_ref), (o_ref, q_ref))):
            turned = dot_nt(eye, product(a[:, at], b[:, at])).astype(BF16)
            s_ref[per * m : per * m + per, which * share : which * share + share, :] = (
                turned.reshape(per, share, B)
            )


def prepare(share, q, k, v, o):
    width = q.shape[1]
    step = 1024
    spec = pl.BlockSpec((B, step), lambda i: (0, i))
    return pl.pallas_call(
        functools.partial(prepare_kernel, share),
        grid=(width // step,),
        in_specs=[spec] * 4,
        out_specs=pl.BlockSpec((step // share, 2 * share, B), lambda i: (i, 0, 0)),
        out_shape=jax.ShapeDtypeStruct((width // share, 2 * share, B), BF16),
        name="prepare",
    )(q, k, v, o)


def swap_matrix():
    rows, cols = iotas((256, 256))
    return one_hot(cols == (rows % 16) * 16 + rows // 16)


def convolve_kernel(
    share, r_ref, f_ref, skip_ref, s_ref, g_ref, taps, xs, gs, ys, zs, x2, g2, t_rows, t_cols
):
    lags = f_ref.shape[0]
    blocks = lags // B
    first = lax.axis_index("dp") * share
    rows, cols = iotas((share, f_ref.shape[1]))
    pick = one_hot(cols == rows + first)
    for m in range(lags // 256):
        at = slice(256 * m, 256 * m + 256)
        taps[:, :, at] = dot_nt(pick, f_ref[at, :].astype(BF16)).reshape(share, 1, 256)
    swap = swap_matrix()

    xs[:, 0:8, :] = jnp.zeros((share, 8, B), F32)
    gs[:, B : B + 8, :] = jnp.zeros((share, 8, B), F32)

    @pl.loop(0, 8)
    def _(i):
        at = pl.multiple_of(i * 16, 16)
        for half in range(share // 16):
            for which in range(2):
                block = r_ref[pl.ds(at, 16), which * share + half * 16 : which * share + half * 16 + 16, :]
                out = dot_nn(swap, block.reshape(256, B)).reshape(16, 16, B)
                if which == 0:
                    xs[half * 16 : half * 16 + 16, pl.ds(at + 8, 16), :] = out
                else:
                    gs[half * 16 : half * 16 + 16, pl.ds(at, 16), :] = out

    x2[0:B, :] = jnp.zeros((B, 2 * B), BF16)
    g2[B : 2 * B, :] = jnp.zeros((B, 2 * B), BF16)
    rows, cols = iotas((B, B))
    flip = one_hot(rows + cols == B - 1)

    @pl.loop(0, share)
    def _(d):
        x = xs[d, 8 : B + 8, :]
        x2[B : 2 * B, 0:B] = x.astype(BF16)
        x2[B : 2 * B, B : 2 * B] = xs[d, 0:B, :].astype(BF16)
        g = gs[d, 0:B, :]
        g2[0:B, 0:B] = g.astype(BF16)
        g2[0:B, B : 2 * B] = gs[d, 8 : B + 8, :].astype(BF16)
        rows, cols = iotas((B, B))
        low = cols >= rows
        before = jnp.zeros((B, B), F32)
        for k in range(blocks):
            line = taps[d, :, B * k : B * k + B]
            turned = pltpu.roll(jnp.broadcast_to(line, (B, B)), 0, 1, stride=1, stride_axis=0)
            t = jnp.where(low, turned, before).astype(BF16)
            t_rows[B * k : B * k + B, :] = t
            t_cols[:, B * k : B * k + B] = t
            before = turned
        gain = skip_ref[first + d]
        y = gain * x
        z = gain * g
        for j in range(blocks // 2):
            y = y + dot_nn(x2[B - 16 * j : 2 * B - 16 * j, :], t_rows[256 * j : 256 * j + 256, :])
            z = z + dot_nt(g2[16 * j : 16 * j + B, :], t_cols[:, 256 * j : 256 * j + 256])
        ys[d] = y.astype(BF16)
        zs[d] = z.astype(BF16)
        x_turned = dot_nt(flip, x2[B : 2 * B, 0:B]).astype(BF16)
        keep = cols + rows >= B - 1
        after = jnp.zeros((B, B), F32)
        for j in reversed(range(blocks // 2)):
            pair = dot_nn(x_turned, g2[16 * j : 16 * j + B, :])
            for k, part in ((2 * j + 1, pair[:, B:]), (2 * j, pair[:, :B])):
                mixed = jnp.where(keep, part, after)
                turned = pltpu.roll(mixed, 1, 1, stride=1, stride_axis=0)
                g_ref[d, :, B * k : B * k + B] = jnp.sum(turned, axis=0, keepdims=True)
                after = part

    @pl.loop(0, 8)
    def _(i):
        at = pl.multiple_of(i * 16, 16)
        for half in range(share // 16):
            for which, ref in enumerate((ys, zs)):
                block = ref[half * 16 : half * 16 + 16, pl.ds(at, 16), :]
                out = dot_nn(swap, block.reshape(256, B)).astype(BF16).reshape(16, 16, B)
                s_ref[pl.ds(at, 16), which * share + half * 16 : which * share + half * 16 + 16, :] = out


def convolve(share, received, filter_taps, skip_gain):
    lags = filter_taps.shape[0]
    vmem = pl.BlockSpec(memory_space=pltpu.VMEM)
    return pl.pallas_call(
        functools.partial(convolve_kernel, share),
        in_specs=[vmem, vmem, pl.BlockSpec(memory_space=pltpu.SMEM)],
        out_specs=[vmem, vmem],
        out_shape=[
            jax.ShapeDtypeStruct(received.shape, BF16),
            jax.ShapeDtypeStruct((share, 1, lags), F32),
        ],
        scratch_shapes=[
            pltpu.VMEM((share, 1, lags), F32),
            pltpu.VMEM((share, B + 8, B), F32),
            pltpu.VMEM((share, B + 8, B), F32),
            pltpu.VMEM((share, B, B), BF16),
            pltpu.VMEM((share, B, B), BF16),
            pltpu.VMEM((2 * B, 2 * B), BF16),
            pltpu.VMEM((2 * B, 2 * B), BF16),
            pltpu.VMEM((lags, B), BF16),
            pltpu.VMEM((B, lags), BF16),
        ],
        compiler_params=pltpu.CompilerParams(vmem_limit_bytes=LIMIT),
        name="convolve",
    )(received, filter_taps, skip_gain)


def finish_kernel(share, r_ref, k_ref, v_ref, o_ref, dq_ref, dk_ref, dv_ref):
    rows, cols = iotas((B, B))
    eye = one_hot(rows == cols)
    per = 256 // share
    for m in range(k_ref.shape[1] // 256):
        at = slice(256 * m, 256 * m + 256)
        conv, back = (
            dot_nt(
                eye,
                r_ref[per * m : per * m + per, which * share : which * share + share, :].reshape(256, B),
            )
            for which in range(2)
        )
        dq_ref[:, at] = (o_ref[:, at].astype(F32) * conv).astype(BF16)
        dk_ref[:, at] = (v_ref[:, at].astype(F32) * back).astype(BF16)
        dv_ref[:, at] = (k_ref[:, at].astype(F32) * back).astype(BF16)


def finish(share, received, k, v, o):
    width = k.shape[1]
    step = 1024
    spec = pl.BlockSpec((B, step), lambda i: (0, i))
    return pl.pallas_call(
        functools.partial(finish_kernel, share),
        grid=(width // step,),
        in_specs=[pl.BlockSpec((step // share, 2 * share, B), lambda i: (i, 0, 0))] + [spec] * 3,
        out_specs=[spec] * 3,
        out_shape=[jax.ShapeDtypeStruct((B, width), BF16)] * 3,
        name="finish",
    )(received, k, v, o)


def per_device(query_rows, key_rows, value_rows, grad_out, filter_taps, skip_gain):
    q, k, v, o = query_rows[0], key_rows[0], value_rows[0], grad_out[0]
    share = q.shape[1] // (lax.axis_size("ctx") * lax.axis_size("dp"))
    every = ("ctx", "dp")
    sent = prepare(share, q, k, v, o)
    received = lax.all_to_all(sent, every, split_axis=0, concat_axis=0, tiled=True)
    back, filter_rows = convolve(share, received, filter_taps, skip_gain)
    filter_rows = filter_rows[:, 0, :]
    returned = lax.all_to_all(back, every, split_axis=0, concat_axis=0, tiled=True)
    dq, dk, dv = finish(share, returned, k, v, o)
    filter_part = lax.all_to_all(filter_rows, "dp", split_axis=1, concat_axis=0, tiled=True)
    return dq[None], dk[None], dv[None], jnp.transpose(filter_part), filter_rows[:, 0]


def solution(mesh):
    rows = P("dp", "ctx", None)
    return jax.shard_map(
        per_device,
        mesh=mesh,
        in_specs=(rows, rows, rows, rows, P(None, "ctx"), P("ctx")),
        out_specs=(rows, rows, rows, P("dp", "ctx"), P(("ctx", "dp"))),
        check_vma=False,
    )
```

profile of v0, /device:TPU:1, one launch (start us, length us, event | category | flops | bytes accessed | tf_op | source)
XLA Modules:
  0.0 140.3 jit_solution(17483585502472787803)
XLA Ops:
  0.6 5.0 %prepare.1 = bf16[128,64,128]{2,1,0:T(8,128)(2,1)} custom-call(bf16[128,4096]{1,0:T(8,128)(2,1)} %bitcast.28, bf16[128,4096]{1,0:T(8,128)(2,1)} %bitcast.19, bf16[128,4096]{1,0:T(8,128)(2,1)} %bitcast.21, bf16[128,4096]{1,0:T(8,128)(2,1)} %bitcast.23), custom_call_target="tpu_custom_call" | custom-call | tf_op jit(solution)/shard_map/prepare/pallas_call | solution.py:56
  5.6 41.2 %all_to_all.29.r_ref = bf16[128,64,128]{2,1,0:T(8,128)(2,1)} all-to-all(bf16[128,64,128]{2,1,0:T(8,128)(2,1)} %prepare.1), channel_id=1, replica_groups=mesh['dp'=8,'ctx'=16] {'ctx','dp'}, dimensions={0} | all-to-all | bytes 4194304 | tf_op jit(solution)/shard_map/all_to_all | solution.py:215
  46.8 40.7 %convolve.1 = (bf16[128,64,128]{2,1,0:T(8,128)(2,1)}, f32[32,1,2048]{2,1,0:T(1,128)}) custom-call(bf16[128,64,128]{2,1,0:T(8,128)(2,1)} %all_to_all.29.r_ref, f32[2048,256]{1,0:T(8,128)} %f_ref.1, f32[256]{0:T(256)} %skip_ref.1), custom_call_target="tpu_custom_call" | custom-call | tf_op jit(solution)/shard_map/convolve/pallas_call | solution.py:154
  87.5 1.6 %reduce = f32[32,2048]{1,0:T(8,128)S(1)} reduce(f32[32,1,2048]{2,1,0:T(1,128)} %get-tuple-element.14, f32[]{:T(128)} %constant.4), dimensions={1}, to_apply=%get-tuple-element.14.reduce_sub_computation | reduce | bytes 524292 | tf_op jit(solution)/shard_map/convolve/pallas_call | solution.py:154
  89.1 9.2 %all_to_all.30 = f32[32,8,256]{2,0,1:T(8,128)S(1)} all-to-all(f32[32,8,256]{2,0,1:T(8,128)S(1)} %bitcast.27), channel_id=1, replica_groups=mesh['dp'=8,'ctx'=16] {'dp'}, dimensions={1} | all-to-all | bytes 524288 | tf_op jit(solution)/shard_map/all_to_all | solution.py:220
  98.4 0.0 copy-start.1
  98.4 5.9 %all-to-all-start.1 = ((bf16[128,64,128]{2,1,0:T(8,128)(2,1)}), bf16[128,64,128]{2,1,0:T(8,128)(2,1)S(1)}, u32[]{:S(2)}, u32[]{:S(2)}) async-start(bf16[128,64,128]{2,1,0:T(8,128)(2,1)} %get-tuple-element.10), calls=%async_computation.1 | async-start | bytes 4194304 | tf_op jit(solution)/shard_map/all_to_all | solution.py:218
  104.3 0.0 copy-done.1
  104.3 0.1 copy.19
  104.4 0.6 slice_reduce_fusion
  105.0 0.8 copy.13
  105.9 28.0 %all-to-all-done.1.r_ref = bf16[128,64,128]{2,1,0:T(8,128)(2,1)S(1)} async-done(((bf16[128,64,128]{2,1,0:T(8,128)(2,1)}), bf16[128,64,128]{2,1,0:T(8,128)(2,1)S(1)}, u32[]{:S(2)}, u32[]{:S(2)}) %all-to-all-start.1) | async-done | bytes 2097184 | tf_op jit(solution)/shard_map/all_to_all | solution.py:218
  133.9 0.0 copy-start
  133.9 1.3 copy-done
  135.3 5.1 %finish.1 = (bf16[128,4096]{1,0:T(8,128)(2,1)}, bf16[128,4096]{1,0:T(8,128)(2,1)}, bf16[128,4096]{1,0:T(8,128)(2,1)}) custom-call(bf16[128,64,128]{2,1,0:T(8,128)(2,1)} %copy-done, bf16[128,4096]{1,0:T(8,128)(2,1)} %bitcast.20, bf16[128,4096]{1,0:T(8,128)(2,1)} %bitcast.22, bf16[128,4096]{1,0:T(8,128)(2,1)} %bitcast.24), custom_call_target="tpu_custom_call" | custom-call | tf_op jit(solution)/shard_map/finish/pallas_call | solution.py:200
  (1 shorter events, 0.0 us)
Async XLA Ops:
  98.4 5.9 %copy-start.1 = (f32[32,1,2048]{2,1,0:T(1,128)S(1)}, f32[32,1,2048]{2,1,0:T(1,128)}, u32[]{:S(2)}) copy-start(f32[32,1,2048]{2,1,0:T(1,128)} %get-tuple-element.14) | copy-start | bytes 786436
  98.4 35.5 %all-to-all-start.1 = ((bf16[128,64,128]{2,1,0:T(8,128)(2,1)}), bf16[128,64,128]{2,1,0:T(8,128)(2,1)S(1)}, u32[]{:S(2)}, u32[]{:S(2)}) async-start(bf16[128,64,128]{2,1,0:T(8,128)(2,1)} %get-tuple-element.10), calls=%async_computation.1 | async-start | bytes 4194304 | tf_op jit(solution)/shard_map/all_to_all | solution.py:218
  133.9 1.3 copy-start
where the time goes:
time: 141 us; the launch traced here: 140 us
  Pallas kernels  50.8 us (36%)
  blocking collectives  50.5 us (36%)
  waiting for transfers between devices  28 us (20%)
  starting transfers between devices  5.9 us (4%)
  local copies, waits for them, and re-layouts  2.91 us (2%)
  other arithmetic  1.57 us (1%)
    all_to_all x1, blocking collectives, per_device(): lax.all_to_all(sent, every, split_axis=0, concat_axis=0, tiled=True)  41.2 us
    pallas_call x1, Pallas kernels, convolve(): pl.pallas_call(functools.partial(convolve_kernel, share), in_specs=[vmem,...  40.7 us
    all_to_all x1, waiting for transfers between devices, per_device(): lax.all_to_all(back, every, split_axis=0, concat_axis=0, tiled=True)  28 us
    all_to_all x1, blocking collectives, per_device(): lax.all_to_all(filter_rows, 'dp', split_axis=1, concat_axis=0, tiled=True)  9.23 us
    all_to_all x1, starting transfers between devices, per_device(): lax.all_to_all(back, every, split_axis=0, concat_axis=0, tiled=True)  5.9 us
    pallas_call x1, Pallas kernels, finish(): pl.pallas_call(functools.partial(finish_kernel, share), grid=(width // st...  5.08 us
    pallas_call x1, Pallas kernels, prepare(): pl.pallas_call(functools.partial(prepare_kernel, share), grid=(width // s...  4.97 us
  transfers between devices with their start and end apart: 1, of which 1 were waited for; matrix products, arithmetic and copies ran while one was open for 1% of the time, Pallas kernels for 0%

commit v1 on v0

v1 whole, which is shorter than its diff:
```python
import functools

import jax
import jax.numpy as jnp
from jax import lax
from jax.experimental import pallas as pl
from jax.experimental.pallas import tpu as pltpu
from jax.sharding import PartitionSpec as P

F32 = jnp.float32
BF16 = jnp.bfloat16
B = 128
LIMIT = 56 * 1024 * 1024


def dot_nn(a, b):
    return lax.dot_general(a, b, (((1,), (0,)), ((), ())), preferred_element_type=F32)


def dot_nt(a, b):
    return lax.dot_general(a, b, (((1,), (1,)), ((), ())), preferred_element_type=F32)


def iotas(shape):
    return (
        lax.broadcasted_iota(jnp.int32, shape, 0),
        lax.broadcasted_iota(jnp.int32, shape, 1),
    )


def one_hot(cond):
    return jnp.where(cond, 1.0, 0.0).astype(BF16)


def product(a, b):
    return (a.astype(F32) * b.astype(F32)).astype(BF16)


UNITS = 4
UNIT = 8
BLOCK = 2 * UNIT
MESH = pl.DeviceIdType.MESH


def prepare_kernel(q_ref, k_ref, v_ref, o_ref, s_ref):
    rows, cols = iotas((256, 256))
    place = one_hot(
        cols == (rows // 8 % 2) * 128 + (rows // 64) * 32 + (rows // 16 % 4) * 8 + rows % 8
    )
    for m in range(q_ref.shape[1] // 256):
        for half in range(2):
            at = slice(256 * m + 128 * half, 256 * m + 128 * half + 128)
            both = jnp.concatenate(
                [product(k_ref[:, at], v_ref[:, at]), product(o_ref[:, at], q_ref[:, at])], axis=1
            )
            turned = dot_nt(place, both).astype(BF16).reshape(4, UNITS, BLOCK, B)
            for u in range(UNITS):
                s_ref[u, 4 * half : 4 * half + 4, m] = turned[:, u]


def prepare(q, k, v, o):
    step = 1024
    spec = pl.BlockSpec((B, step), lambda i: (0, i))
    return pl.pallas_call(
        prepare_kernel,
        grid=(q.shape[1] // step,),
        in_specs=[spec] * 4,
        out_specs=pl.BlockSpec((UNITS, 8, 4, BLOCK, B), lambda i: (0, i // 2, i % 2, 0, 0)),
        out_shape=jax.ShapeDtypeStruct((UNITS, 16, 8, BLOCK, B), BF16),
        name="prepare",
    )(q, k, v, o)


def exchange_kernel(
    s_ref, f_ref, skip_ref, r_ref, h_ref, first_ref,
    mid_in, whole_in, out, mid_out, g_out, taps, xs, gs, ys, zs, gu, x2, g2, t_rows, t_cols, swap, flip,
    send, recv, g_send, g_recv, own,
):
    lags = f_ref.shape[0]
    blocks = lags // B
    ctx, dp = lax.axis_index("ctx"), lax.axis_index("dp")
    x_high, zc = ctx // 8, ctx % 8
    plane = x_high * 8 + dp
    x, y, z, core = x_high * 2 + dp // 4, dp % 4, zc // 2, zc % 2

    def plane_peer(n):
        there_x, there_y = (x + n % 4) % 4, (y + n // 4) % 4
        there_dp = (there_x % 2) * 4 + there_y
        device = {"ctx": (there_x // 2) * 8 + zc, "dp": there_dp}
        return device, (there_x // 2) * 8 + there_dp

    def line_peer(n):
        there = ((z + n % 4) % 4) * 2 + (core + n // 4) % 2
        return {"ctx": x_high * 8 + there, "dp": dp}, there

    barrier = pltpu.get_barrier_semaphore()

    @pl.loop(1, 16)
    def _(n):
        pl.semaphore_signal(barrier, 1, device_id=plane_peer(n)[0], device_id_type=MESH)

    @pl.loop(1, 8)
    def _(n):
        pl.semaphore_signal(barrier, 1, device_id=line_peer(n)[0], device_id_type=MESH)

    pl.semaphore_wait(barrier, 22)

    def send_all(phase, u, count, peer, source, target, mine):
        pltpu.make_async_copy(source(mine), target, own.at[phase, u]).start()

        @pl.loop(1, count)
        def _(n):
            device, index = peer(n)
            pltpu.make_async_remote_copy(
                src_ref=source(index),
                dst_ref=target,
                send_sem=send.at[phase, u],
                recv_sem=recv.at[phase, u],
                device_id=device,
                device_id_type=MESH,
            ).start()

    def arrived(phase, u, where, mine, count):
        pltpu.make_async_copy(where.at[u, mine], where.at[u, mine], own.at[phase, u]).wait()
        some = where.at[u, pl.ds(0, count - 1)]
        pltpu.make_async_copy(some, some, recv.at[phase, u]).wait()

    def in_first(u):
        send_all(0, u, 16, plane_peer, lambda i: s_ref.at[u, i], mid_in.at[u, plane], plane)

    def in_second(u):
        arrived(0, u, mid_in, plane, 16)
        send_all(1, u, 8, line_peer, lambda i: mid_in.at[u, :, i], whole_in.at[u, zc], zc)

    def out_first(u):
        send_all(2, u, 8, line_peer, lambda i: out.at[u, i], mid_out.at[u, zc], zc)

    def out_second(u):
        arrived(2, u, mid_out, zc, 8)
        send_all(3, u, 16, plane_peer, lambda i: mid_out.at[u, :, i], r_ref.at[u, plane], plane)

    for u in range(UNITS):
        in_first(u)

    share = UNITS * UNIT
    first = dp * share
    rows, cols = iotas((share, f_ref.shape[1]))
    pick = one_hot(cols == rows + first)
    for m in range(lags // 256):
        at = slice(256 * m, 256 * m + 256)
        taps[:, :, at] = dot_nt(pick, f_ref[at, :].astype(BF16)).reshape(share, 1, 256)
    rows, cols = iotas((256, 256))
    swap[...] = one_hot(cols == (rows % 16) * 16 + rows // 16)
    rows, cols = iotas((B, B))
    flip[...] = one_hot(rows + cols == B - 1)
    xs[:, 0:8, :] = jnp.zeros((UNIT, 8, B), F32)
    gs[:, B : B + 8, :] = jnp.zeros((UNIT, 8, B), F32)
    x2[0:B, :] = jnp.zeros((B, 2 * B), BF16)
    g2[B : 2 * B, :] = jnp.zeros((B, 2 * B), BF16)

    in_second(0)
    in_second(1)

    def unpack(u):
        @pl.loop(0, 8)
        def _(i):
            rows = dot_nn(swap[...], whole_in[u, i].reshape(256, B)).reshape(2, UNIT, 2, 8, B)
            at = pl.multiple_of(i * 8, 8)
            for high in range(2):
                xs[:, pl.ds(at + 64 * high + 8, 8), :] = rows[0, :, high]
                gs[:, pl.ds(at + 64 * high, 8), :] = rows[1, :, high]

    def pack(u):
        @pl.loop(0, 8)
        def _(i):
            at = pl.multiple_of(i * 8, 8)
            parts = [
                jnp.concatenate([ref[:, pl.ds(at, 8), :], ref[:, pl.ds(at + 64, 8), :]], axis=1)
                for ref in (ys, zs)
            ]
            rows = jnp.concatenate(parts, axis=0).astype(BF16).reshape(256, B)
            out[u, i] = dot_nn(swap[...], rows).astype(BF16).reshape(16, BLOCK, B)

        at = pl.multiple_of(u * UNIT, UNIT)
        filter_rows = gu[...].reshape(UNIT, lags)
        for i in range(8):
            g_out[i, pl.ds(at, UNIT), :] = filter_rows[:, 256 * i : 256 * i + 256]

    def channel(u, d):
        x = xs[d, 8 : B + 8, :]
        x2[B : 2 * B, 0:B] = x.astype(BF16)
        x2[B : 2 * B, B : 2 * B] = xs[d, 0:B, :].astype(BF16)
        g = gs[d, 0:B, :]
        g2[0:B, 0:B] = g.astype(BF16)
        g2[0:B, B : 2 * B] = gs[d, 8 : B + 8, :].astype(BF16)
        rows, cols = iotas((B, B))
        low = cols >= rows
        before = jnp.zeros((B, B), F32)
        for k in range(blocks):
            line = taps[u * UNIT + d, :, B * k : B * k + B]
            turned = pltpu.roll(jnp.broadcast_to(line, (B, B)), 0, 1, stride=1, stride_axis=0)
            t = jnp.where(low, turned, before).astype(BF16)
            t_rows[B * k : B * k + B, :] = t
            t_cols[:, B * k : B * k + B] = t
            before = turned
        gain = skip_ref[first + u * UNIT + d]
        y = gain * x
        z = gain * g
        for j in range(blocks // 2):
            y = y + dot_nn(x2[B - 16 * j : 2 * B - 16 * j, :], t_rows[256 * j : 256 * j + 256, :])
            z = z + dot_nt(g2[16 * j : 16 * j + B, :], t_cols[:, 256 * j : 256 * j + 256])
        ys[d] = y
        zs[d] = z
        x_turned = dot_nt(flip[...], x2[B : 2 * B, 0:B]).astype(BF16)
        keep = cols + rows >= B - 1
        after = jnp.zeros((B, B), F32)
        for j in reversed(range(blocks // 2)):
            pair = dot_nn(x_turned, g2[16 * j : 16 * j + B, :])
            for k, part in ((2 * j + 1, pair[:, B:]), (2 * j, pair[:, :B])):
                mixed = jnp.where(keep, part, after)
                turned = pltpu.roll(mixed, 1, 1, stride=1, stride_axis=0)
                gu[d, :, B * k : B * k + B] = jnp.sum(turned, axis=0, keepdims=True)
                after = part

    @pl.loop(0, 2 * UNITS)
    def _(step):
        u, half = step // 2, step % 2

        @pl.when(half == 0)
        def _():
            arrived(1, u, whole_in, zc, 8)
            unpack(u)

        @pl.loop(0, UNIT // 2)
        def _(d):
            channel(u, half * (UNIT // 2) + d)

        @pl.when(jnp.logical_and(half == 0, u < UNITS - 2))
        def _():
            in_second(u + 2)

        @pl.when(jnp.logical_and(half == 0, u > 0))
        def _():
            out_second(u - 1)

        @pl.when(half == 1)
        def _():
            pack(u)
            out_first(u)

    def g_copy(n):
        there = (dp + n) % 8
        return pltpu.make_async_remote_copy(
            src_ref=g_out.at[there],
            dst_ref=h_ref.at[dp],
            send_sem=g_send,
            recv_sem=g_recv,
            device_id={"ctx": ctx, "dp": there},
            device_id_type=MESH,
        )

    own_g = pltpu.make_async_copy(g_out.at[dp], h_ref.at[dp], own.at[4, 0])
    own_g.start()

    @pl.loop(1, 8)
    def _(n):
        g_copy(n).start()

    first_ref[...] = g_out[0, :, 0:B]
    out_second(UNITS - 1)
    for u in range(UNITS):
        arrived(3, u, r_ref, plane, 16)
    own_g.wait()
    for sem in (g_recv, g_send):
        pltpu.make_async_copy(h_ref.at[pl.ds(0, 7)], h_ref.at[pl.ds(0, 7)], sem).wait()
    for u in range(UNITS):
        for phase, some in ((0, mid_in.at[u, 0:15]), (1, whole_in.at[u, 0:7]), (2, mid_out.at[u, 0:7]), (3, r_ref.at[u, 0:15])):
            pltpu.make_async_copy(some, some, send.at[phase, u]).wait()


def exchange(sent, filter_taps, skip_gain):
    lags = filter_taps.shape[0]
    share = UNITS * UNIT
    vmem = pl.BlockSpec(memory_space=pltpu.VMEM)
    anywhere = pl.BlockSpec(memory_space=pl.ANY)
    return pl.pallas_call(
        exchange_kernel,
        in_specs=[anywhere, vmem, pl.BlockSpec(memory_space=pltpu.SMEM)],
        out_specs=[anywhere, anywhere, vmem],
        out_shape=[
            jax.ShapeDtypeStruct((UNITS, 16, 8, BLOCK, B), BF16),
            jax.ShapeDtypeStruct((8, share, lags // 8), F32),
            jax.ShapeDtypeStruct((share, B), F32),
        ],
        scratch_shapes=[
            pltpu.VMEM((UNITS, 16, 8, BLOCK, B), BF16),
            pltpu.VMEM((UNITS, 8, 16, BLOCK, B), BF16),
            pltpu.VMEM((UNITS, 8, 16, BLOCK, B), BF16),
            pltpu.VMEM((UNITS, 8, 16, BLOCK, B), BF16),
            pltpu.VMEM((8, share, lags // 8), F32),
            pltpu.VMEM((share, 1, lags), F32),
            pltpu.VMEM((UNIT, B + 8, B), F32),
            pltpu.VMEM((UNIT, B + 8, B), F32),
            pltpu.VMEM((UNIT, B, B), F32),
            pltpu.VMEM((UNIT, B, B), F32),
            pltpu.VMEM((UNIT, 1, lags), F32),
            pltpu.VMEM((2 * B, 2 * B), BF16),
            pltpu.VMEM((2 * B, 2 * B), BF16),
            pltpu.VMEM((lags, B), BF16),
            pltpu.VMEM((B, lags), BF16),
            pltpu.VMEM((256, 256), BF16),
            pltpu.VMEM((B, B), BF16),
            pltpu.SemaphoreType.DMA((4, UNITS)),
            pltpu.SemaphoreType.DMA((4, UNITS)),
            pltpu.SemaphoreType.DMA,
            pltpu.SemaphoreType.DMA,
            pltpu.SemaphoreType.DMA((5, UNITS)),
        ],
        compiler_params=pltpu.CompilerParams(
            collective_id=0, has_side_effects=True, vmem_limit_bytes=LIMIT
        ),
        name="exchange",
    )(sent, filter_taps, skip_gain)


def finish_kernel(r_ref, k_ref, v_ref, o_ref, dq_ref, dk_ref, dv_ref):
    rows, cols = iotas((256, 256))
    place = one_hot(
        cols == (rows // 8 % 4) * 64 + (rows // 32 % 4) * 16 + (rows // 128) * 8 + rows % 8
    )
    rows, cols = iotas((B, B))
    eye = one_hot(rows == cols)
    for m in range(k_ref.shape[1] // 256):
        for half in range(2):
            at = slice(256 * m + 128 * half, 256 * m + 128 * half + 128)
            mixed = r_ref[:, 4 * half : 4 * half + 4, m].reshape(256, B)
            both = dot_nt(eye, dot_nn(place, mixed).astype(BF16))
            conv, back = both[:, :B], both[:, B:]
            dq_ref[:, at] = (o_ref[:, at].astype(F32) * conv).astype(BF16)
            dk_ref[:, at] = (v_ref[:, at].astype(F32) * back).astype(BF16)
            dv_ref[:, at] = (k_ref[:, at].astype(F32) * back).astype(BF16)


def finish(received, k, v, o):
    width = k.shape[1]
    step = 1024
    spec = pl.BlockSpec((B, step), lambda i: (0, i))
    return pl.pallas_call(
        finish_kernel,
        grid=(width // step,),
        in_specs=[pl.BlockSpec((UNITS, 8, 4, BLOCK, B), lambda i: (0, i // 2, i % 2, 0, 0))] + [spec] * 3,
        out_specs=[spec] * 3,
        out_shape=[jax.ShapeDtypeStruct((B, width), BF16)] * 3,
        name="finish",
    )(received, k, v, o)


def per_device(query_rows, key_rows, value_rows, grad_out, filter_taps, skip_gain):
    q, k, v, o = query_rows[0], key_rows[0], value_rows[0], grad_out[0]
    sent = prepare(q, k, v, o)
    returned, filter_rows, first_lags = exchange(sent, filter_taps, skip_gain)
    dq, dk, dv = finish(returned, k, v, o)
    filter_part = jnp.transpose(filter_rows.reshape(-1, filter_rows.shape[2]))
    return dq[None], dk[None], dv[None], filter_part, first_lags[:, 0]


def solution(mesh):
    rows = P("dp", "ctx", None)
    return jax.shard_map(
        per_device,
        mesh=mesh,
        in_specs=(rows, rows, rows, rows, P(None, "ctx"), P("ctx")),
        out_specs=(rows, rows, rows, P("dp", "ctx"), P(("ctx", "dp"))),
        check_vma=False,
    )
```

time: 141 us -> 115 us (0.82)
  Pallas kernels: 50.8 us -> 111 us
  blocking collectives: 50.5 us -> 0 us
  waiting for transfers between devices: 28 us -> 0 us
  starting transfers between devices: 5.9 us -> 0 us
  other arithmetic: 1.57 us -> 0 us
    pallas_call x3, Pallas kernels: 50.8 us -> 111 us  [the longest x1 96.3 us: exchange(): pl.pallas_call(exchange_kernel, in_specs=[anywhere, vmem, pl.BlockSpec(me...]
    all_to_all x2 -> x0, blocking collectives: 50.5 us -> none  [the longest x1 41.2 us: per_device(): lax.all_to_all(sent, every, split_axis=0, concat_axis=0, tiled=True)]
    all_to_all x1 -> x0, waiting for transfers between devices: 28 us -> none  [per_device(): lax.all_to_all(back, every, split_axis=0, concat_axis=0, tiled=True)]
    all_to_all x1 -> x0, starting transfers between devices: 5.9 us -> none  [per_device(): lax.all_to_all(back, every, split_axis=0, concat_axis=0, tiled=True)]
    unnamed x6 -> x0, local copies, waits for them, and re-layouts: 2.27 us -> none
    reshape x0 -> x1, local copies, waits for them, and re-layouts: none -> 1.79 us  [per_device(): filter_part = jnp.transpose(filter_rows.reshape(-1, filter_rows.shape[2]))]
    pallas_call x1 -> x0, other arithmetic: 1.57 us -> none  [convolve(): pl.pallas_call(functools.partial(convolve_kernel, share), in_specs=[vmem,...]
  transfers between devices with their start and end apart: 1 -> 0, of which waited for: 1 -> 0; matrix products, arithmetic and copies ran while one was open for 1% -> 0% of each run, Pallas kernels for 0% -> 0%
where the time goes in v1:
time: 115 us
  Pallas kernels  111 us (97%)
  local copies, waits for them, and re-layouts  3.13 us (3%)
    pallas_call x1, Pallas kernels, exchange(): pl.pallas_call(exchange_kernel, in_specs=[anywhere, vmem, pl.BlockSpec(me...  96.3 us
    pallas_call x1, Pallas kernels, finish(): pl.pallas_call(finish_kernel, grid=(width // step,), in_specs=[pl.BlockSp...  9.9 us
    pallas_call x1, Pallas kernels, prepare(): pl.pallas_call(prepare_kernel, grid=(q.shape[1] // step,), in_specs=[spec...  5.21 us

profile of v1, /device:TPU:1, one launch (start us, length us, event | category | flops | bytes accessed | tf_op | source)
XLA Modules:
  0.0 115.2 jit_solution(766719406031841568)
XLA Ops:
  0.6 5.2 %prepare.1.s_ref = bf16[4,16,8,16,128]{4,3,2,1,0:T(8,128)(2,1)} custom-call(bf16[128,4096]{1,0:T(8,128)(2,1)} %bitcast.15, bf16[128,4096]{1,0:T(8,128)(2,1)} %bitcast.9, bf16[128,4096]{1,0:T(8,128)(2,1)} %bitcast.11, bf16[128,4096]{1,0:T(8,128)(2,1)} %bitcast.13), custom_call_target="tpu_custom_call" | custom-call | tf_op jit(solution)/shard_map/prepare/pallas_call | solution.py:64
  5.8 96.3 %exchange.1 = (bf16[4,16,8,16,128]{4,3,2,1,0:T(8,128)(2,1)}, f32[8,32,256]{2,1,0:T(8,128)}, f32[32,128]{1,0:T(8,128)}) custom-call(bf16[4,16,8,16,128]{4,3,2,1,0:T(8,128)(2,1)} %prepare.1.s_ref, f32[2048,256]{1,0:T(8,128)} %f_ref.1, f32[256]{0:T(256)} %skip_ref.1), custom_call_target="tpu_custom_call" | custom-call | tf_op jit(solution)/shard_map/exchange/pallas_call | solution.py:286
  102.1 1.8 %copy.12 = f32[256,256]{0,1:T(8,128)} copy(f32[256,256]{1,0:T(8,128)} %bitcast.17) | data formatting | bytes 524288 | tf_op jit(solution)/shard_map/reshape | solution.py:363
  103.9 1.3 %slice_reduce_fusion = f32[32]{0:T(128)} fusion(f32[32,128]{1,0:T(8,128)} %get-tuple-element.16), kind=kLoop, calls=%fused_computation | loop fusion | bytes 256 | tf_op jit(solution)/shard_map/slice | solution.py:364
  105.3 9.9 %finish.1 = (bf16[128,4096]{1,0:T(8,128)(2,1)}, bf16[128,4096]{1,0:T(8,128)(2,1)}, bf16[128,4096]{1,0:T(8,128)(2,1)}) custom-call(bf16[4,16,8,16,128]{4,3,2,1,0:T(8,128)(2,1)} %get-tuple-element.11.r_ref, bf16[128,4096]{1,0:T(8,128)(2,1)} %bitcast.10, bf16[128,4096]{1,0:T(8,128)(2,1)} %bitcast.12, bf16[128,4096]{1,0:T(8,128)(2,1)} %bitcast.14), custom_call_target="tpu_custom_call" | custom-call | tf_op jit(solution)/shard_map/finish/pallas_call | solution.py:348

commit v2 on v1

v2 whole, which is shorter than its diff:
```python
import functools

import jax
import jax.numpy as jnp
from jax import lax
from jax.experimental import pallas as pl
from jax.experimental.pallas import tpu as pltpu
from jax.sharding import PartitionSpec as P

F32 = jnp.float32
BF16 = jnp.bfloat16
B = 128
LIMIT = 56 * 1024 * 1024


def dot_nn(a, b):
    return lax.dot_general(a, b, (((1,), (0,)), ((), ())), preferred_element_type=F32)


def dot_nt(a, b):
    return lax.dot_general(a, b, (((1,), (1,)), ((), ())), preferred_element_type=F32)


def iotas(shape):
    return (
        lax.broadcasted_iota(jnp.int32, shape, 0),
        lax.broadcasted_iota(jnp.int32, shape, 1),
    )


def one_hot(cond):
    return jnp.where(cond, 1.0, 0.0).astype(BF16)


def product(a, b):
    return (a.astype(F32) * b.astype(F32)).astype(BF16)


UNITS = 4
UNIT = 8
BLOCK = 2 * UNIT
CHIPS = 64
MESH = pl.DeviceIdType.MESH


def prepare_kernel(q_ref, k_ref, v_ref, o_ref, s_ref):
    rows, cols = iotas((256, 256))
    place = one_hot(
        cols == (rows // 8 % 2) * 128 + (rows // 64) * 32 + (rows // 16 % 4) * 8 + rows % 8
    )
    for m in range(q_ref.shape[1] // 256):
        for half in range(2):
            at = slice(256 * m + 128 * half, 256 * m + 128 * half + 128)
            both = jnp.concatenate(
                [product(k_ref[:, at], v_ref[:, at]), product(o_ref[:, at], q_ref[:, at])], axis=1
            )
            turned = dot_nt(place, both).astype(BF16).reshape(4, UNITS, BLOCK, B)
            for u in range(UNITS):
                s_ref[u, m % 2, half, :, m // 2] = turned[:, u]


def prepare(q, k, v, o):
    step = 2048
    spec = pl.BlockSpec((B, step), lambda i: (0, i))
    return pl.pallas_call(
        prepare_kernel,
        grid=(q.shape[1] // step,),
        in_specs=[spec] * 4,
        out_specs=pl.BlockSpec(
            (UNITS, 2, 2, 4, step // 512, BLOCK, B),
            lambda i: (0, 0, i * step // 2048, 0, i % (2048 // step), 0, 0),
        ),
        out_shape=jax.ShapeDtypeStruct((UNITS, 2, 4, 4, 4, BLOCK, B), BF16),
        name="prepare",
    )(q, k, v, o)


def exchange_kernel(
    s_ref, f_any, skip_ref, r_ref, h_ref, first_ref,
    f_ref, going, come, staged, leaving,
    g_out, taps, xs, gs, ys, zs, gu, x2s, g2s, t_rows_s, t_cols_s, swap, flip,
    own_sems, hand_send, hand_recv, send, recv, stay, g_send, g_recv, g_own, f_sem,
):
    lags = f_ref.shape[0]
    blocks = lags // B
    ctx, dp = lax.axis_index("ctx"), lax.axis_index("dp")
    core = ctx % 2
    x, y, z = (ctx // 8) * 2 + dp // 4, dp % 4, (ctx // 2) % 4
    chip = x * 16 + y * 4 + z
    mate = {"ctx": ctx + 1 - 2 * core, "dp": dp}

    def peer(n):
        m = (n * 27) % CHIPS
        x_there, y_there, z_there = (x + m // 16) % 4, (y + m // 4) % 4, (z + m) % 4
        device = {
            "ctx": (x_there // 2) * 8 + z_there * 2 + core,
            "dp": (x_there % 2) * 4 + y_there,
        }
        return device, x_there * 16 + y_there * 4 + z_there

    def remote(source, target, sems, device):
        pltpu.make_async_remote_copy(
            src_ref=source,
            dst_ref=target,
            send_sem=sems[0],
            recv_sem=sems[1],
            device_id=device,
            device_id_type=MESH,
        ).start()

    def wait_for(some, sem):
        pltpu.make_async_copy(some, some, sem).wait()

    barrier = pltpu.get_barrier_semaphore()
    pl.semaphore_signal(barrier, 1, device_id=mate, device_id_type=MESH)

    @pl.loop(1, CHIPS)
    def _(n):
        pl.semaphore_signal(barrier, 1, device_id=peer(n)[0], device_id_type=MESH)

    def own_copy(u):
        return pltpu.make_async_copy(s_ref.at[u, core], going.at[u, :, core], own_sems.at[u])

    filter_copy = pltpu.make_async_copy(f_any, f_ref, f_sem)
    for u in range(UNITS):
        own_copy(u).start()
    filter_copy.start()
    pl.semaphore_wait(barrier, CHIPS)
    for u in range(UNITS):
        remote(s_ref.at[u, 1 - core], going.at[u, :, core], (hand_send.at[0, u], hand_recv.at[0, u]), mate)

    def spread(way, u, source, target):
        @pl.loop(1, CHIPS)
        def _(n):
            device, there = peer(n)
            remote(source.at[u, there], target.at[u, chip], (send.at[way, u], recv.at[way, u]), device)

        pltpu.make_async_copy(source.at[u, chip], target.at[u, chip], stay.at[way, u]).start()

    def gathered(way, u, target):
        wait_for(target.at[u, chip], stay.at[way, u])
        wait_for(target.at[u, 0 : CHIPS - 1], recv.at[way, u])

    @pl.loop(0, UNITS)
    def _(u):
        own_copy(u).wait()
        wait_for(going.at[u, :, 1 - core], hand_recv.at[0, u])
        spread(0, u, going, come)

    share = UNITS * UNIT
    first = dp * share
    filter_copy.wait()
    rows, cols = iotas((share, f_ref.shape[1]))
    pick = one_hot(cols == rows + first)
    for m in range(lags // 256):
        at = slice(256 * m, 256 * m + 256)
        taps[:, :, at] = dot_nt(pick, f_ref[at, :].astype(BF16)).reshape(share, 1, 256)
    rows, cols = iotas((256, 256))
    swap[...] = one_hot(cols == (rows % 16) * 16 + rows // 16)
    rows, cols = iotas((B, B))
    flip[...] = one_hot(rows + cols == B - 1)
    xs[:, 0:8, :] = jnp.zeros((UNIT, 8, B), F32)
    gs[:, B : B + 8, :] = jnp.zeros((UNIT, 8, B), F32)
    x2s[:, 0:B, :] = jnp.zeros((2, B, 2 * B), BF16)
    g2s[:, B : 2 * B, :] = jnp.zeros((2, B, 2 * B), BF16)

    def unpack(u):
        @pl.loop(0, 4)
        def _(iz):
            for ic in range(2):
                block = jnp.concatenate(
                    [come[u, pl.ds(4 * i + iz, 1), ic] for i in range(16)], axis=0
                ).reshape(256, B)
                rows = dot_nn(swap[...], block).reshape(2, UNIT, 2, 8, B)
                at = pl.multiple_of((iz * 2 + ic) * 8, 8)
                for high in range(2):
                    xs[:, pl.ds(at + 64 * high + 8, 8), :] = rows[0, :, high]
                    gs[:, pl.ds(at + 64 * high, 8), :] = rows[1, :, high]

    def pack(u):
        @pl.loop(0, 4)
        def _(iz):
            for ic in range(2):
                at = pl.multiple_of((iz * 2 + ic) * 8, 8)
                parts = [
                    jnp.concatenate([ref[:, pl.ds(at, 8), :], ref[:, pl.ds(at + 64, 8), :]], axis=1)
                    for ref in (ys, zs)
                ]
                rows = jnp.concatenate(parts, axis=0).astype(BF16).reshape(256, B)
                turned = dot_nn(swap[...], rows).astype(BF16).reshape(16, BLOCK, B)

                @pl.when(core == ic)
                def _():
                    for i in range(16):
                        leaving[u, 4 * i + iz, ic] = turned[i]

                @pl.when(core != ic)
                def _():
                    for i in range(16):
                        staged[u, 4 * i + iz] = turned[i]

        at = pl.multiple_of(u * UNIT, UNIT)
        filter_rows = gu[...].reshape(UNIT, lags)
        for i in range(8):
            g_out[i, pl.ds(at, UNIT), :] = filter_rows[:, 256 * i : 256 * i + 256]

    def send_filter(u):
        at = pl.multiple_of(u * UNIT, UNIT)
        rows = pl.ds(at, UNIT)
        pltpu.make_async_copy(g_out.at[dp, rows], h_ref.at[dp, rows], g_own.at[u]).start()

        @pl.loop(1, 8)
        def _(n):
            there = (dp + n) % 8
            remote(
                g_out.at[there, rows],
                h_ref.at[dp, rows],
                (g_send.at[u], g_recv.at[u]),
                {"ctx": ctx, "dp": there},
            )

    def hand_out(u):
        remote(staged.at[u], leaving.at[u, :, core], (hand_send.at[1, u], hand_recv.at[1, u]), mate)

    def send_out(u):
        wait_for(leaving.at[u, :, 1 - core], hand_recv.at[1, u])
        spread(1, u, leaving, r_ref)

    def channel(u, d, way):
        x2, g2, t_rows, t_cols = x2s.at[way], g2s.at[way], t_rows_s.at[way], t_cols_s.at[way]
        x = xs[d, 8 : B + 8, :]
        x2[B : 2 * B, 0:B] = x.astype(BF16)
        x2[B : 2 * B, B : 2 * B] = xs[d, 0:B, :].astype(BF16)
        g = gs[d, 0:B, :]
        g2[0:B, 0:B] = g.astype(BF16)
        g2[0:B, B : 2 * B] = gs[d, 8 : B + 8, :].astype(BF16)
        rows, cols = iotas((B, B))
        low = cols >= rows
        before = jnp.zeros((B, B), F32)
        for k in range(blocks):
            line = taps[u * UNIT + d, :, B * k : B * k + B]
            turned = pltpu.roll(jnp.broadcast_to(line, (B, B)), 0, 1, stride=1, stride_axis=0)
            t = jnp.where(low, turned, before).astype(BF16)
            t_rows[B * k : B * k + B, :] = t
            t_cols[:, B * k : B * k + B] = t
            before = turned
        gain = skip_ref[first + u * UNIT + d]
        y = gain * x
        z = gain * g
        for j in range(blocks // 2):
            y = y + dot_nn(x2[B - 16 * j : 2 * B - 16 * j, :], t_rows[256 * j : 256 * j + 256, :])
            z = z + dot_nt(g2[16 * j : 16 * j + B, :], t_cols[:, 256 * j : 256 * j + 256])
        ys[d] = y
        zs[d] = z
        x_turned = dot_nt(flip[...], x2[B : 2 * B, 0:B]).astype(BF16)
        keep = cols + rows >= B - 1
        after = jnp.zeros((B, B), F32)
        for j in reversed(range(blocks // 2)):
            pair = dot_nn(x_turned, g2[16 * j : 16 * j + B, :])
            for k, part in ((2 * j + 1, pair[:, B:]), (2 * j, pair[:, :B])):
                mixed = jnp.where(keep, part, after)
                turned = pltpu.roll(mixed, 1, 1, stride=1, stride_axis=0)
                gu[d, :, B * k : B * k + B] = jnp.sum(turned, axis=0, keepdims=True)
                after = part

    @pl.loop(0, 4 * UNITS)
    def _(step):
        u, part = step // 4, step % 4

        @pl.when(part == 0)
        def _():
            gathered(0, u, come)
            unpack(u)

        for d in range(2):
            channel(u, part * 2 + d, d)

        @pl.when(jnp.logical_and(part == 0, u > 0))
        def _():
            send_out(u - 1)

        @pl.when(part == 3)
        def _():
            pack(u)
            hand_out(u)
            send_filter(u)

    last = UNITS - 1
    send_out(last)
    first_ref[...] = g_out[0, :, 0:B]
    for u in range(UNITS):
        gathered(1, u, r_ref)
        rows = pl.ds(UNIT * u, UNIT)
        pltpu.make_async_copy(g_out.at[dp, rows], h_ref.at[dp, rows], g_own.at[u]).wait()
        some = h_ref.at[0:7, rows]
        for sem in (g_send, g_recv):
            wait_for(some, sem.at[u])
        wait_for(staged.at[u], hand_send.at[0, u])
        wait_for(staged.at[u], hand_send.at[1, u])
        wait_for(come.at[u, 0 : CHIPS - 1], send.at[0, u])
        wait_for(come.at[u, 0 : CHIPS - 1], send.at[1, u])


def exchange(sent, filter_taps, skip_gain):
    sent = sent.reshape(UNITS, 2, CHIPS, BLOCK, B)
    lags = filter_taps.shape[0]
    share = UNITS * UNIT
    vmem = pl.BlockSpec(memory_space=pltpu.VMEM)
    anywhere = pl.BlockSpec(memory_space=pl.ANY)
    return pl.pallas_call(
        exchange_kernel,
        in_specs=[anywhere, anywhere, pl.BlockSpec(memory_space=pltpu.SMEM)],
        out_specs=[anywhere, anywhere, vmem],
        out_shape=[
            jax.ShapeDtypeStruct((UNITS, CHIPS, 2, BLOCK, B), BF16),
            jax.ShapeDtypeStruct((8, share, lags // 8), F32),
            jax.ShapeDtypeStruct((share, B), F32),
        ],
        scratch_shapes=[
            pltpu.VMEM(filter_taps.shape, F32),
            pltpu.VMEM((UNITS, CHIPS, 2, BLOCK, B), BF16),
            pltpu.VMEM((UNITS, CHIPS, 2, BLOCK, B), BF16),
            pltpu.VMEM((UNITS, CHIPS, BLOCK, B), BF16),
            pltpu.VMEM((UNITS, CHIPS, 2, BLOCK, B), BF16),
            pltpu.VMEM((8, share, lags // 8), F32),
            pltpu.VMEM((share, 1, lags), F32),
            pltpu.VMEM((UNIT, B + 8, B), F32),
            pltpu.VMEM((UNIT, B + 8, B), F32),
            pltpu.VMEM((UNIT, B, B), F32),
            pltpu.VMEM((UNIT, B, B), F32),
            pltpu.VMEM((UNIT, 1, lags), F32),
            pltpu.VMEM((2, 2 * B, 2 * B), BF16),
            pltpu.VMEM((2, 2 * B, 2 * B), BF16),
            pltpu.VMEM((2, lags, B), BF16),
            pltpu.VMEM((2, B, lags), BF16),
            pltpu.VMEM((256, 256), BF16),
            pltpu.VMEM((B, B), BF16),
            pltpu.SemaphoreType.DMA((UNITS,)),
            pltpu.SemaphoreType.DMA((2, UNITS)),
            pltpu.SemaphoreType.DMA((2, UNITS)),
            pltpu.SemaphoreType.DMA((2, UNITS)),
            pltpu.SemaphoreType.DMA((2, UNITS)),
            pltpu.SemaphoreType.DMA((2, UNITS)),
            pltpu.SemaphoreType.DMA((UNITS,)),
            pltpu.SemaphoreType.DMA((UNITS,)),
            pltpu.SemaphoreType.DMA((UNITS,)),
            pltpu.SemaphoreType.DMA,
        ],
        compiler_params=pltpu.CompilerParams(
            collective_id=0, has_side_effects=True, vmem_limit_bytes=LIMIT
        ),
        name="exchange",
    )(sent, filter_taps, skip_gain)


def finish_kernel(r_ref, k_ref, v_ref, o_ref, dq_ref, dk_ref, dv_ref):
    rows, cols = iotas((B, B))
    eye = one_hot(rows == cols)
    for m in range(k_ref.shape[1] // 256):
        for half in range(2):
            at = slice(256 * m + 128 * half, 256 * m + 128 * half + 128)
            mixed = r_ref[:, half, :, m // 2, m % 2].astype(F32)
            sorted_rows = jnp.concatenate(
                [
                    mixed[u, dp, which * UNIT : which * UNIT + UNIT]
                    for which in range(2)
                    for dp in range(4)
                    for u in range(UNITS)
                ],
                axis=0,
            ).astype(BF16)
            both = dot_nt(eye, sorted_rows)
            conv, back = both[:, :B], both[:, B:]
            dq_ref[:, at] = (o_ref[:, at].astype(F32) * conv).astype(BF16)
            dk_ref[:, at] = (v_ref[:, at].astype(F32) * back).astype(BF16)
            dv_ref[:, at] = (k_ref[:, at].astype(F32) * back).astype(BF16)


def finish(received, k, v, o):
    width = k.shape[1]
    step = 2048
    spec = pl.BlockSpec((B, step), lambda i: (0, i))
    return pl.pallas_call(
        finish_kernel,
        grid=(width // step,),
        in_specs=[
            pl.BlockSpec(
                (UNITS, 2, 4, step // 512, 2, BLOCK, B),
                lambda i: (0, i * step // 2048, 0, i % (2048 // step), 0, 0, 0),
            )
        ]
        + [spec] * 3,
        out_specs=[spec] * 3,
        out_shape=[jax.ShapeDtypeStruct((B, width), BF16)] * 3,
        name="finish",
    )(received, k, v, o)


def per_device(query_rows, key_rows, value_rows, grad_out, filter_taps, skip_gain):
    q, k, v, o = query_rows[0], key_rows[0], value_rows[0], grad_out[0]
    sent = prepare(q, k, v, o)
    returned, filter_rows, first_lags = exchange(sent, filter_taps, skip_gain)
    returned = returned.reshape(UNITS, 4, 4, 4, 2, BLOCK, B)
    dq, dk, dv = finish(returned, k, v, o)
    filter_part = jnp.transpose(filter_rows.reshape(-1, filter_rows.shape[2]))
    return dq[None], dk[None], dv[None], filter_part, first_lags[:, 0]


def solution(mesh):
    rows = P("dp", "ctx", None)
    return jax.shard_map(
        per_device,
        mesh=mesh,
        in_specs=(rows, rows, rows, rows, P(None, "ctx"), P("ctx")),
        out_specs=(rows, rows, rows, P("dp", "ctx"), P(("ctx", "dp"))),
        check_vma=False,
    )
```

time: 115 us -> 93.3 us (0.81)
  Pallas kernels: 111 us -> 89.3 us
    pallas_call x1, Pallas kernels: 96.3 us -> 80.8 us  [exchange(): pl.pallas_call(exchange_kernel, in_specs=[anywhere, anywhere, pl.BlockSpe...]
    pallas_call x1, Pallas kernels: 9.9 us -> 4.26 us  [finish(): pl.pallas_call(finish_kernel, grid=(width // step,), in_specs=[pl.BlockSp...]
where the time goes in v2:
time: 93.3 us; the launch traced here: 93.1 us
  Pallas kernels  89.3 us (96%)
  local copies, waits for them, and re-layouts  3.13 us (3%)
    pallas_call x1, Pallas kernels, exchange(): pl.pallas_call(exchange_kernel, in_specs=[anywhere, anywhere, pl.BlockSpe...  80.8 us
    pallas_call x1, Pallas kernels, finish(): pl.pallas_call(finish_kernel, grid=(width // step,), in_specs=[pl.BlockSp...  4.26 us
    pallas_call x1, Pallas kernels, prepare(): pl.pallas_call(prepare_kernel, grid=(q.shape[1] // step,), in_specs=[spec...  4.2 us

profile of v2, /device:TPU:1, one launch (start us, length us, event | category | flops | bytes accessed | tf_op | source)
XLA Modules:
  0.0 93.1 jit_solution(6078716656623171446)
XLA Ops:
  0.6 4.2 %prepare.1 = bf16[4,2,4,4,4,16,128]{6,5,4,3,2,1,0:T(8,128)(2,1)} custom-call(bf16[128,4096]{1,0:T(8,128)(2,1)} %bitcast.19, bf16[128,4096]{1,0:T(8,128)(2,1)} %bitcast.12, bf16[128,4096]{1,0:T(8,128)(2,1)} %bitcast.14, bf16[128,4096]{1,0:T(8,128)(2,1)} %bitcast.16), custom_call_target="tpu_custom_call" | custom-call | tf_op jit(solution)/shard_map/prepare/pallas_call | solution.py:65
  4.8 80.8 %exchange.1 = (bf16[4,64,2,16,128]{4,3,2,1,0:T(8,128)(2,1)}, f32[8,32,256]{2,1,0:T(8,128)}, f32[32,128]{1,0:T(8,128)}) custom-call(bf16[4,2,64,16,128]{4,3,2,1,0:T(8,128)(2,1)} %bitcast.11, f32[2048,256]{1,0:T(8,128)} %f_any.1, f32[256]{0:T(256)} %skip_ref.1), custom_call_target="tpu_custom_call" | custom-call | tf_op jit(solution)/shard_map/exchange/pallas_call | solution.py:310
  85.7 1.8 %copy.12 = f32[256,256]{0,1:T(8,128)} copy(f32[256,256]{1,0:T(8,128)} %bitcast.21) | data formatting | bytes 524288 | tf_op jit(solution)/shard_map/reshape | solution.py:405
  87.5 1.3 %slice_reduce_fusion = f32[32]{0:T(128)} fusion(f32[32,128]{1,0:T(8,128)} %get-tuple-element.16), kind=kLoop, calls=%fused_computation | loop fusion | bytes 256 | tf_op jit(solution)/shard_map/slice | solution.py:406
  88.8 4.3 %finish.1 = (bf16[128,4096]{1,0:T(8,128)(2,1)}, bf16[128,4096]{1,0:T(8,128)(2,1)}, bf16[128,4096]{1,0:T(8,128)(2,1)}) custom-call(bf16[4,4,4,4,2,16,128]{6,5,4,3,2,1,0:T(8,128)(2,1)} %bitcast.18, bf16[128,4096]{1,0:T(8,128)(2,1)} %bitcast.13, bf16[128,4096]{1,0:T(8,128)(2,1)} %bitcast.15, bf16[128,4096]{1,0:T(8,128)(2,1)} %bitcast.17), custom_call_target="tpu_custom_call" | custom-call | tf_op jit(solution)/shard_map/finish/pallas_call | solution.py:383

commit v3 on v2

--- a/solution.py
+++ b/solution.py
@@ -39,6 +39,7 @@
 UNITS = 4
 UNIT = 8
 BLOCK = 2 * UNIT
+PADDED = B + 16
 CHIPS = 64
 MESH = pl.DeviceIdType.MESH
 
@@ -78,7 +79,7 @@
 def exchange_kernel(
     s_ref, f_any, skip_ref, r_ref, h_ref, first_ref,
     f_ref, going, come, staged, leaving,
-    g_out, taps, xs, gs, ys, zs, gu, x2s, g2s, t_rows_s, t_cols_s, swap, flip,
+    g_out, taps, xs, gs, ys, zs, gu, x2s, g2s, g2ms, t_rows_s, t_cols_s, flip,
     own_sems, hand_send, hand_recv, send, recv, stay, g_send, g_recv, g_own, f_sem,
 ):
     lags = f_ref.shape[0]
@@ -90,11 +91,14 @@
     mate = {"ctx": ctx + 1 - 2 * core, "dp": dp}
 
     def peer(n):
-        m = (n * 27) % CHIPS
-        x_there, y_there, z_there = (x + m // 16) % 4, (y + m // 4) % 4, (z + m) % 4
+        m = lax.rem(n * 27, CHIPS)
+        x_there = lax.rem(x + lax.div(m, 16), 4)
+        y_there = lax.rem(y + lax.div(m, 4), 4)
+        z_there = lax.rem(z + m, 4)
+        x_high = lax.div(x_there, 2)
         device = {
-            "ctx": (x_there // 2) * 8 + z_there * 2 + core,
-            "dp": (x_there % 2) * 4 + y_there,
+            "ctx": x_high * 8 + z_there * 2 + core,
+            "dp": (x_there - 2 * x_high) * 4 + y_there,
         }
         return device, x_there * 16 + y_there * 4 + z_there
 
@@ -155,49 +159,44 @@
     for m in range(lags // 256):
         at = slice(256 * m, 256 * m + 256)
         taps[:, :, at] = dot_nt(pick, f_ref[at, :].astype(BF16)).reshape(share, 1, 256)
-    rows, cols = iotas((256, 256))
-    swap[...] = one_hot(cols == (rows % 16) * 16 + rows // 16)
     rows, cols = iotas((B, B))
     flip[...] = one_hot(rows + cols == B - 1)
-    xs[:, 0:8, :] = jnp.zeros((UNIT, 8, B), F32)
-    gs[:, B : B + 8, :] = jnp.zeros((UNIT, 8, B), F32)
+    for d in range(UNIT):
+        xs[PADDED * d : PADDED * d + 8, :] = jnp.zeros((8, B), F32)
+        gs[PADDED * d + B : PADDED * d + PADDED, :] = jnp.zeros((16, B), F32)
     x2s[:, 0:B, :] = jnp.zeros((2, B, 2 * B), BF16)
     g2s[:, B : 2 * B, :] = jnp.zeros((2, B, 2 * B), BF16)
+    g2ms[:, B : 2 * B, :] = jnp.zeros((2, B, 2 * B), BF16)
 
     def unpack(u):
         @pl.loop(0, 4)
         def _(iz):
             for ic in range(2):
-                block = jnp.concatenate(
-                    [come[u, pl.ds(4 * i + iz, 1), ic] for i in range(16)], axis=0
-                ).reshape(256, B)
-                rows = dot_nn(swap[...], block).reshape(2, UNIT, 2, 8, B)
-                at = pl.multiple_of((iz * 2 + ic) * 8, 8)
-                for high in range(2):
-                    xs[:, pl.ds(at + 64 * high + 8, 8), :] = rows[0, :, high]
-                    gs[:, pl.ds(at + 64 * high, 8), :] = rows[1, :, high]
+                for i in range(16):
+                    block = come[u, 4 * i + iz, ic].astype(F32)
+                    row = (i // 8) * 64 + iz * 16 + ic * 8 + i % 8
+                    xs[pl.ds(row + 8, UNIT, PADDED), :] = block[:UNIT]
+                    gs[pl.ds(row, UNIT, PADDED), :] = block[UNIT:]
 
     def pack(u):
         @pl.loop(0, 4)
         def _(iz):
             for ic in range(2):
-                at = pl.multiple_of((iz * 2 + ic) * 8, 8)
-                parts = [
-                    jnp.concatenate([ref[:, pl.ds(at, 8), :], ref[:, pl.ds(at + 64, 8), :]], axis=1)
-                    for ref in (ys, zs)
-                ]
-                rows = jnp.concatenate(parts, axis=0).astype(BF16).reshape(256, B)
-                turned = dot_nn(swap[...], rows).astype(BF16).reshape(16, BLOCK, B)
+                blocks_out = []
+                for i in range(16):
+                    row = (i // 8) * 64 + iz * 16 + ic * 8 + i % 8
+                    pair = [ref[pl.ds(row, UNIT, B), :] for ref in (ys, zs)]
+                    blocks_out.append(jnp.concatenate(pair, axis=0).astype(BF16))
 
                 @pl.when(core == ic)
                 def _():
                     for i in range(16):
-                        leaving[u, 4 * i + iz, ic] = turned[i]
+                        leaving[u, 4 * i + iz, ic] = blocks_out[i]
 
                 @pl.when(core != ic)
                 def _():
                     for i in range(16):
-                        staged[u, 4 * i + iz] = turned[i]
+                        staged[u, 4 * i + iz] = blocks_out[i]
 
         at = pl.multiple_of(u * UNIT, UNIT)
         filter_rows = gu[...].reshape(UNIT, lags)
@@ -227,13 +226,16 @@
         spread(1, u, leaving, r_ref)
 
     def channel(u, d, way):
-        x2, g2, t_rows, t_cols = x2s.at[way], g2s.at[way], t_rows_s.at[way], t_cols_s.at[way]
-        x = xs[d, 8 : B + 8, :]
+        x2, g2, g2m, t_rows, t_cols = (
+            ref.at[way] for ref in (x2s, g2s, g2ms, t_rows_s, t_cols_s)
+        )
+        base = pl.multiple_of(d * PADDED, 8)
+        x = xs[pl.ds(base + 8, B), :]
         x2[B : 2 * B, 0:B] = x.astype(BF16)
-        x2[B : 2 * B, B : 2 * B] = xs[d, 0:B, :].astype(BF16)
-        g = gs[d, 0:B, :]
+        x2[B : 2 * B, B : 2 * B] = xs[pl.ds(base, B), :].astype(BF16)
+        g = gs[pl.ds(base, B), :]
         g2[0:B, 0:B] = g.astype(BF16)
-        g2[0:B, B : 2 * B] = gs[d, 8 : B + 8, :].astype(BF16)
+        g2[0:B, B : 2 * B] = gs[pl.ds(base + 8, B), :].astype(BF16)
         rows, cols = iotas((B, B))
         low = cols >= rows
         before = jnp.zeros((B, B), F32)
@@ -250,16 +252,25 @@
         for j in range(blocks // 2):
             y = y + dot_nn(x2[B - 16 * j : 2 * B - 16 * j, :], t_rows[256 * j : 256 * j + 256, :])
             z = z + dot_nt(g2[16 * j : 16 * j + B, :], t_cols[:, 256 * j : 256 * j + 256])
-        ys[d] = y
-        zs[d] = z
+        at = pl.multiple_of(d * B, B)
+        ys[pl.ds(at, B), :] = y
+        zs[pl.ds(at, B), :] = z
+        moved = pltpu.roll(gs[pl.ds(base, PADDED), :], B // 2, 1)
+        _, lanes = iotas((B + 8, B))
+        moved = jnp.where(lanes < B // 2, moved[: B + 8], moved[8:])
+        g2m[0:B, 0:B] = moved[:B].astype(BF16)
+        g2m[0:B, B : 2 * B] = moved[8:].astype(BF16)
         x_turned = dot_nt(flip[...], x2[B : 2 * B, 0:B]).astype(BF16)
-        keep = cols + rows >= B - 1
-        after = jnp.zeros((B, B), F32)
+        x_turned = jnp.concatenate([x_turned[B // 2 :], x_turned[: B // 2]], axis=1)
+        rows, cols = iotas((B // 2, B))
+        keep = cols + rows >= B // 2 - 1
+        after = jnp.zeros((B // 2, B), F32)
         for j in reversed(range(blocks // 2)):
-            pair = dot_nn(x_turned, g2[16 * j : 16 * j + B, :])
+            at = slice(16 * j, 16 * j + B)
+            pair = dot_nn(x_turned, jnp.concatenate([g2[at, :], g2m[at, :]], axis=0))
             for k, part in ((2 * j + 1, pair[:, B:]), (2 * j, pair[:, :B])):
                 mixed = jnp.where(keep, part, after)
-                turned = pltpu.roll(mixed, 1, 1, stride=1, stride_axis=0)
+                turned = pltpu.roll(mixed, B // 2 + 1, 1, stride=1, stride_axis=0)
                 gu[d, :, B * k : B * k + B] = jnp.sum(turned, axis=0, keepdims=True)
                 after = part
 
@@ -324,16 +335,16 @@
             pltpu.VMEM((UNITS, CHIPS, 2, BLOCK, B), BF16),
             pltpu.VMEM((8, share, lags // 8), F32),
             pltpu.VMEM((share, 1, lags), F32),
-            pltpu.VMEM((UNIT, B + 8, B), F32),
-            pltpu.VMEM((UNIT, B + 8, B), F32),
-            pltpu.VMEM((UNIT, B, B), F32),
-            pltpu.VMEM((UNIT, B, B), F32),
+            pltpu.VMEM((UNIT * PADDED, B), F32),
+            pltpu.VMEM((UNIT * PADDED, B), F32),
+            pltpu.VMEM((UNIT * B, B), F32),
+            pltpu.VMEM((UNIT * B, B), F32),
             pltpu.VMEM((UNIT, 1, lags), F32),
+            pltpu.VMEM((2, 2 * B, 2 * B), BF16),
             pltpu.VMEM((2, 2 * B, 2 * B), BF16),
             pltpu.VMEM((2, 2 * B, 2 * B), BF16),
             pltpu.VMEM((2, lags, B), BF16),
             pltpu.VMEM((2, B, lags), BF16),
-            pltpu.VMEM((256, 256), BF16),
             pltpu.VMEM((B, B), BF16),
             pltpu.SemaphoreType.DMA((UNITS,)),
             pltpu.SemaphoreType.DMA((2, UNITS)),
@@ -353,7 +364,12 @@
     )(sent, filter_taps, skip_gain)
 
 
-def finish_kernel(r_ref, k_ref, v_ref, o_ref, dq_ref, dk_ref, dv_ref):
+def finish_kernel(r_ref, k_ref, v_ref, o_ref, h_ref, first_ref, dq_ref, dk_ref, dv_ref, df_ref, ds_ref):
+    @pl.when(pl.program_id(0) == 0)
+    def _():
+        df_ref[...] = jnp.transpose(h_ref[...])
+        ds_ref[...] = jnp.transpose(first_ref[...])[0:1]
+
     rows, cols = iotas((B, B))
     eye = one_hot(rows == cols)
     for m in range(k_ref.shape[1] // 256):
@@ -376,7 +392,8 @@
             dv_ref[:, at] = (k_ref[:, at].astype(F32) * back).astype(BF16)
 
 
-def finish(received, k, v, o):
+def finish(received, k, v, o, filter_rows, first_lags):
+    channels, lags = filter_rows.shape
     width = k.shape[1]
     step = 2048
     spec = pl.BlockSpec((B, step), lambda i: (0, i))
@@ -389,11 +406,17 @@
                 lambda i: (0, i * step // 2048, 0, i % (2048 // step), 0, 0, 0),
             )
         ]
-        + [spec] * 3,
-        out_specs=[spec] * 3,
-        out_shape=[jax.ShapeDtypeStruct((B, width), BF16)] * 3,
+        + [spec] * 3
+        + [pl.BlockSpec((channels, lags), lambda i: (0, 0)), pl.BlockSpec(first_lags.shape, lambda i: (0, 0))],
+        out_specs=[spec] * 3
+        + [pl.BlockSpec((lags, channels), lambda i: (0, 0)), pl.BlockSpec((1, first_lags.shape[0]), lambda i: (0, 0))],
+        out_shape=[jax.ShapeDtypeStruct((B, width), BF16)] * 3
+        + [
+            jax.ShapeDtypeStruct((lags, channels), F32),
+            jax.ShapeDtypeStruct((1, first_lags.shape[0]), F32),
+        ],
         name="finish",
-    )(received, k, v, o)
+    )(received, k, v, o, filter_rows, first_lags)
 
 
 def per_device(query_rows, key_rows, value_rows, grad_out, filter_taps, skip_gain):
@@ -401,9 +424,9 @@
     sent = prepare(q, k, v, o)
     returned, filter_rows, first_lags = exchange(sent, filter_taps, skip_gain)
     returned = returned.reshape(UNITS, 4, 4, 4, 2, BLOCK, B)
-    dq, dk, dv = finish(returned, k, v, o)
-    filter_part = jnp.transpose(filter_rows.reshape(-1, filter_rows.shape[2]))
-    return dq[None], dk[None], dv[None], filter_part, first_lags[:, 0]
+    filter_rows = filter_rows.reshape(-1, filter_rows.shape[2])
+    dq, dk, dv, d_filter, d_skip = finish(returned, k, v, o, filter_rows, first_lags)
+    return dq[None], dk[None], dv[None], d_filter, d_skip[0]
 
 
 def solution(mesh):

time: 93.3 us -> 79.6 us (0.85)
  Pallas kernels: 89.3 us -> 78.8 us
  local copies, waits for them, and re-layouts: 3.13 us -> 0 us
    pallas_call x1, Pallas kernels: 80.8 us -> 70.3 us  [exchange(): pl.pallas_call(exchange_kernel, in_specs=[anywhere, anywhere, pl.BlockSpe...]
    reshape x1 -> x0, local copies, waits for them, and re-layouts: 1.79 us -> none  [per_device(): filter_part = jnp.transpose(filter_rows.reshape(-1, filter_rows.shape[2]))]
    slice x1 -> x0, local copies, waits for them, and re-layouts: 1.34 us -> none  [per_device(): return (dq[None], dk[None], dv[None], filter_part, first_lags[:, 0])]
where the time goes in v3:
time: 79.6 us; the launch traced here: 79.5 us
  Pallas kernels  78.8 us (99%)
    pallas_call x1, Pallas kernels, exchange(): pl.pallas_call(exchange_kernel, in_specs=[anywhere, anywhere, pl.BlockSpe...  70.3 us
    pallas_call x1, Pallas kernels, finish(): pl.pallas_call(finish_kernel, grid=(width // step,), in_specs=[pl.BlockSp...  4.41 us
    pallas_call x1, Pallas kernels, prepare(): pl.pallas_call(prepare_kernel, grid=(q.shape[1] // step,), in_specs=[spec...  4.16 us

profile of v3, /device:TPU:1, one launch (start us, length us, event | category | flops | bytes accessed | tf_op | source)
XLA Modules:
  0.0 79.5 jit_solution(12345763155466175316)
XLA Ops:
  0.6 4.2 %prepare.1 = bf16[4,2,4,4,4,16,128]{6,5,4,3,2,1,0:T(8,128)(2,1)} custom-call(bf16[128,4096]{1,0:T(8,128)(2,1)} %bitcast.19, bf16[128,4096]{1,0:T(8,128)(2,1)} %bitcast.12, bf16[128,4096]{1,0:T(8,128)(2,1)} %bitcast.14, bf16[128,4096]{1,0:T(8,128)(2,1)} %bitcast.16), custom_call_target="tpu_custom_call" | custom-call | tf_op jit(solution)/shard_map/prepare/pallas_call | solution.py:66
  4.8 70.3 %exchange.1 = (bf16[4,64,2,16,128]{4,3,2,1,0:T(8,128)(2,1)}, f32[8,32,256]{2,1,0:T(8,128)}, f32[32,128]{1,0:T(8,128)}) custom-call(bf16[4,2,64,16,128]{4,3,2,1,0:T(8,128)(2,1)} %bitcast.11, f32[2048,256]{1,0:T(8,128)} %f_any.1, f32[256]{0:T(256)} %skip_ref.1), custom_call_target="tpu_custom_call" | custom-call | tf_op jit(solution)/shard_map/exchange/pallas_call | solution.py:321
  75.1 4.4 %finish.1 = (bf16[128,4096]{1,0:T(8,128)(2,1)}, bf16[128,4096]{1,0:T(8,128)(2,1)}, bf16[128,4096]{1,0:T(8,128)(2,1)}, f32[256,256]{1,0:T(8,128)}, f32[1,32]{1,0:T(1,128)}) custom-call(bf16[4,4,4,4,2,16,128]{6,5,4,3,2,1,0:T(8,128)(2,1)} %bitcast.18, bf16[128,4096]{1,0:T(8,128)(2,1)} %bitcast.13, bf16[128,4096]{1,0:T(8,128)(2,1)} %bitcast.15, ...), custom_call_target="tpu_custom_call" | custom-call | tf_op jit(solution)/shard_map/finish/pallas_call | solution.py:400

commit v4 on v3

--- a/solution.py
+++ b/solution.py
@@ -44,43 +44,11 @@
 MESH = pl.DeviceIdType.MESH
 
 
-def prepare_kernel(q_ref, k_ref, v_ref, o_ref, s_ref):
-    rows, cols = iotas((256, 256))
-    place = one_hot(
-        cols == (rows // 8 % 2) * 128 + (rows // 64) * 32 + (rows // 16 % 4) * 8 + rows % 8
-    )
-    for m in range(q_ref.shape[1] // 256):
-        for half in range(2):
-            at = slice(256 * m + 128 * half, 256 * m + 128 * half + 128)
-            both = jnp.concatenate(
-                [product(k_ref[:, at], v_ref[:, at]), product(o_ref[:, at], q_ref[:, at])], axis=1
-            )
-            turned = dot_nt(place, both).astype(BF16).reshape(4, UNITS, BLOCK, B)
-            for u in range(UNITS):
-                s_ref[u, m % 2, half, :, m // 2] = turned[:, u]
-
-
-def prepare(q, k, v, o):
-    step = 2048
-    spec = pl.BlockSpec((B, step), lambda i: (0, i))
-    return pl.pallas_call(
-        prepare_kernel,
-        grid=(q.shape[1] // step,),
-        in_specs=[spec] * 4,
-        out_specs=pl.BlockSpec(
-            (UNITS, 2, 2, 4, step // 512, BLOCK, B),
-            lambda i: (0, 0, i * step // 2048, 0, i % (2048 // step), 0, 0),
-        ),
-        out_shape=jax.ShapeDtypeStruct((UNITS, 2, 4, 4, 4, BLOCK, B), BF16),
-        name="prepare",
-    )(q, k, v, o)
-
-
 def exchange_kernel(
-    s_ref, f_any, skip_ref, r_ref, h_ref, first_ref,
-    f_ref, going, come, staged, leaving,
-    g_out, taps, xs, gs, ys, zs, gu, x2s, g2s, g2ms, t_rows_s, t_cols_s, flip,
-    own_sems, hand_send, hand_recv, send, recv, stay, g_send, g_recv, g_own, f_sem,
+    q_any, k_any, v_any, o_any, f_any, skip_ref, r_ref, h_ref, first_ref,
+    q_ref, k_ref, v_ref, o_ref, f_ref, going, prepared, come, staged, leaving,
+    g_out, taps, xs, gs, ys, zs, gu, x2s, g2s, g2ms, t_rows_s, t_cols_s, flip, turn,
+    load_sems, hand_send, hand_recv, send, recv, stay, g_send, g_recv, g_own, f_sem,
 ):
     lags = f_ref.shape[0]
     blocks = lags // B
@@ -115,6 +83,21 @@
     def wait_for(some, sem):
         pltpu.make_async_copy(some, some, sem).wait()
 
+    half_width = q_ref.shape[1] // 2
+
+    def load(half):
+        at = slice(half * half_width, half * half_width + half_width)
+        return [
+            pltpu.make_async_copy(any_ref.at[:, at], ref.at[:, at], load_sems.at[half, i])
+            for i, (any_ref, ref) in enumerate(
+                ((k_any, k_ref), (v_any, v_ref), (o_any, o_ref), (q_any, q_ref))
+            )
+        ]
+
+    for half in range(2):
+        for copy in load(half):
+            copy.start()
+
     barrier = pltpu.get_barrier_semaphore()
     pl.semaphore_signal(barrier, 1, device_id=mate, device_id_type=MESH)
 
@@ -122,16 +105,48 @@
     def _(n):
         pl.semaphore_signal(barrier, 1, device_id=peer(n)[0], device_id_type=MESH)
 
-    def own_copy(u):
-        return pltpu.make_async_copy(s_ref.at[u, core], going.at[u, :, core], own_sems.at[u])
-
     filter_copy = pltpu.make_async_copy(f_any, f_ref, f_sem)
-    for u in range(UNITS):
-        own_copy(u).start()
     filter_copy.start()
+
+    rows, cols = iotas((256, 256))
+    turn[...] = one_hot(
+        cols == (rows // 8 % 2) * 128 + (rows // 64) * 32 + (rows // 16 % 4) * 8 + rows % 8
+    )
+
+    def prepare(x_upper):
+        @pl.loop(0, 4)
+        def _(iz):
+            for ic in range(2):
+                for x_lower in range(2):
+                    start = x_upper * half_width + (iz * 2 + ic) * 256 + x_lower * B
+                    at = pl.ds(pl.multiple_of(start, B), B)
+                    both = jnp.concatenate(
+                        [product(k_ref[:, at], v_ref[:, at]), product(o_ref[:, at], q_ref[:, at])],
+                        axis=1,
+                    )
+                    turned = dot_nt(turn[...], both).astype(BF16).reshape(4, UNITS, BLOCK, B)
+                    corner = x_upper * 32 + x_lower * 16 + iz
+
+                    @pl.when(core == ic)
+                    def _():
+                        for there_y in range(4):
+                            for u in range(UNITS):
+                                going[u, corner + 4 * there_y, ic] = turned[there_y, u]
+
+                    @pl.when(core != ic)
+                    def _():
+                        for there_y in range(4):
+                            for u in range(UNITS):
+                                prepared[u, corner + 4 * there_y] = turned[there_y, u]
+
+    for half in range(2):
+        for copy in load(half):
+            copy.wait()
+        prepare(half)
+
     pl.semaphore_wait(barrier, CHIPS)
     for u in range(UNITS):
-        remote(s_ref.at[u, 1 - core], going.at[u, :, core], (hand_send.at[0, u], hand_recv.at[0, u]), mate)
+        remote(prepared.at[u], going.at[u, :, core], (hand_send.at[0, u], hand_recv.at[0, u]), mate)
 
     def spread(way, u, source, target):
         @pl.loop(1, CHIPS)
@@ -147,7 +162,6 @@
 
     @pl.loop(0, UNITS)
     def _(u):
-        own_copy(u).wait()
         wait_for(going.at[u, :, 1 - core], hand_recv.at[0, u])
         spread(0, u, going, come)
 
@@ -312,15 +326,14 @@
         wait_for(come.at[u, 0 : CHIPS - 1], send.at[1, u])
 
 
-def exchange(sent, filter_taps, skip_gain):
-    sent = sent.reshape(UNITS, 2, CHIPS, BLOCK, B)
+def exchange(q, k, v, o, filter_taps, skip_gain):
     lags = filter_taps.shape[0]
     share = UNITS * UNIT
     vmem = pl.BlockSpec(memory_space=pltpu.VMEM)
     anywhere = pl.BlockSpec(memory_space=pl.ANY)
     return pl.pallas_call(
         exchange_kernel,
-        in_specs=[anywhere, anywhere, pl.BlockSpec(memory_space=pltpu.SMEM)],
+        in_specs=[anywhere] * 5 + [pl.BlockSpec(memory_space=pltpu.SMEM)],
         out_specs=[anywhere, anywhere, vmem],
         out_shape=[
             jax.ShapeDtypeStruct((UNITS, CHIPS, 2, BLOCK, B), BF16),
@@ -328,8 +341,10 @@
             jax.ShapeDtypeStruct((share, B), F32),
         ],
         scratch_shapes=[
+            *[pltpu.VMEM(q.shape, BF16)] * 4,
             pltpu.VMEM(filter_taps.shape, F32),
             pltpu.VMEM((UNITS, CHIPS, 2, BLOCK, B), BF16),
+            pltpu.VMEM((UNITS, CHIPS, BLOCK, B), BF16),
             pltpu.VMEM((UNITS, CHIPS, 2, BLOCK, B), BF16),
             pltpu.VMEM((UNITS, CHIPS, BLOCK, B), BF16),
             pltpu.VMEM((UNITS, CHIPS, 2, BLOCK, B), BF16),
@@ -346,7 +361,8 @@
             pltpu.VMEM((2, lags, B), BF16),
             pltpu.VMEM((2, B, lags), BF16),
             pltpu.VMEM((B, B), BF16),
-            pltpu.SemaphoreType.DMA((UNITS,)),
+            pltpu.VMEM((256, 256), BF16),
+            pltpu.SemaphoreType.DMA((2, 4)),
             pltpu.SemaphoreType.DMA((2, UNITS)),
             pltpu.SemaphoreType.DMA((2, UNITS)),
             pltpu.SemaphoreType.DMA((2, UNITS)),
@@ -361,7 +377,7 @@
             collective_id=0, has_side_effects=True, vmem_limit_bytes=LIMIT
         ),
         name="exchange",
-    )(sent, filter_taps, skip_gain)
+    )(q, k, v, o, filter_taps, skip_gain)
 
 
 def finish_kernel(r_ref, k_ref, v_ref, o_ref, h_ref, first_ref, dq_ref, dk_ref, dv_ref, df_ref, ds_ref):
@@ -421,8 +437,7 @@
 
 def per_device(query_rows, key_rows, value_rows, grad_out, filter_taps, skip_gain):
     q, k, v, o = query_rows[0], key_rows[0], value_rows[0], grad_out[0]
-    sent = prepare(q, k, v, o)
-    returned, filter_rows, first_lags = exchange(sent, filter_taps, skip_gain)
+    returned, filter_rows, first_lags = exchange(q, k, v, o, filter_taps, skip_gain)
     returned = returned.reshape(UNITS, 4, 4, 4, 2, BLOCK, B)
     filter_rows = filter_rows.reshape(-1, filter_rows.shape[2])
     dq, dk, dv, d_filter, d_skip = finish(returned, k, v, o, filter_rows, first_lags)

time: 79.6 us -> 78.1 us (0.981)
  Pallas kernels: 78.8 us -> 77.4 us
    pallas_call x2 -> x1, Pallas kernels: 74.4 us -> 73 us  [exchange(): pl.pallas_call(exchange_kernel, in_specs=[anywhere] * 5 + [pl.BlockSpec(m...]
where the time goes in v4:
time: 78.1 us; the launch traced here: 78 us
  Pallas kernels  77.4 us (99%)
    pallas_call x1, Pallas kernels, exchange(): pl.pallas_call(exchange_kernel, in_specs=[anywhere] * 5 + [pl.BlockSpec(m...  73 us
    pallas_call x1, Pallas kernels, finish(): pl.pallas_call(finish_kernel, grid=(width // step,), in_specs=[pl.BlockSp...  4.4 us

profile of v4, /device:TPU:1, one launch (start us, length us, event | category | flops | bytes accessed | tf_op | source)
XLA Modules:
  0.0 78.0 jit_solution(7071456363111999732)
XLA Ops:
  0.6 73.0 %exchange.1 = (bf16[4,64,2,16,128]{4,3,2,1,0:T(8,128)(2,1)}, f32[8,32,256]{2,1,0:T(8,128)}, f32[32,128]{1,0:T(8,128)}) custom-call(bf16[128,4096]{1,0:T(8,128)(2,1)} %bitcast.17, bf16[128,4096]{1,0:T(8,128)(2,1)} %bitcast.10, bf16[128,4096]{1,0:T(8,128)(2,1)} %bitcast.12, bf16[128,4096]{1,0:T(8,128)(2,1)} %bitcast.14, f32[2048,256]{1,0:T(8,128)} %f_any.1, ...), custom_call_target="tpu_custom_call" | custom-call | tf_op jit(solution)/shard_map/exchange/pallas_call | solution.py:334
  73.6 4.4 %finish.1 = (bf16[128,4096]{1,0:T(8,128)(2,1)}, bf16[128,4096]{1,0:T(8,128)(2,1)}, bf16[128,4096]{1,0:T(8,128)(2,1)}, f32[256,256]{1,0:T(8,128)}, f32[1,32]{1,0:T(1,128)}) custom-call(bf16[4,4,4,4,2,16,128]{6,5,4,3,2,1,0:T(8,128)(2,1)} %bitcast.16, bf16[128,4096]{1,0:T(8,128)(2,1)} %bitcast.11, bf16[128,4096]{1,0:T(8,128)(2,1)} %bitcast.13, ...), custom_call_target="tpu_custom_call" | custom-call | tf_op jit(solution)/shard_map/finish/pallas_call | solution.py:416

commit v5 on v4

--- a/solution.py
+++ b/solution.py
@@ -46,7 +46,7 @@
 
 def exchange_kernel(
     q_any, k_any, v_any, o_any, f_any, skip_ref, r_ref, h_ref, first_ref,
-    q_ref, k_ref, v_ref, o_ref, f_ref, going, prepared, come, staged, leaving,
+    q_ref, k_ref, v_ref, o_ref, f_ref, going, come, leaving,
     g_out, taps, xs, gs, ys, zs, gu, x2s, g2s, g2ms, t_rows_s, t_cols_s, flip, turn,
     load_sems, hand_send, hand_recv, send, recv, stay, g_send, g_recv, g_own, f_sem,
 ):
@@ -57,6 +57,9 @@
     x, y, z = (ctx // 8) * 2 + dp // 4, dp % 4, (ctx // 2) % 4
     chip = x * 16 + y * 4 + z
     mate = {"ctx": ctx + 1 - 2 * core, "dp": dp}
+
+    def slot(ic):
+        return ic + lax.rem(core + ic, 2) * (2 - ic)
 
     def peer(n):
         m = lax.rem(n * 27, CHIPS)
@@ -127,17 +130,9 @@
                     turned = dot_nt(turn[...], both).astype(BF16).reshape(4, UNITS, BLOCK, B)
                     corner = x_upper * 32 + x_lower * 16 + iz
 
-                    @pl.when(core == ic)
-                    def _():
-                        for there_y in range(4):
-                            for u in range(UNITS):
-                                going[u, corner + 4 * there_y, ic] = turned[there_y, u]
-
-                    @pl.when(core != ic)
-                    def _():
-                        for there_y in range(4):
-                            for u in range(UNITS):
-                                prepared[u, corner + 4 * there_y] = turned[there_y, u]
+                    for there_y in range(4):
+                        for u in range(UNITS):
+                            going[u, corner + 4 * there_y, slot(ic)] = turned[there_y, u]
 
     for half in range(2):
         for copy in load(half):
@@ -146,15 +141,15 @@
 
     pl.semaphore_wait(barrier, CHIPS)
     for u in range(UNITS):
-        remote(prepared.at[u], going.at[u, :, core], (hand_send.at[0, u], hand_recv.at[0, u]), mate)
+        remote(going.at[u, :, 2], going.at[u, :, core], (hand_send.at[0, u], hand_recv.at[0, u]), mate)
 
     def spread(way, u, source, target):
         @pl.loop(1, CHIPS)
         def _(n):
             device, there = peer(n)
-            remote(source.at[u, there], target.at[u, chip], (send.at[way, u], recv.at[way, u]), device)
-
-        pltpu.make_async_copy(source.at[u, chip], target.at[u, chip], stay.at[way, u]).start()
+            remote(source.at[u, there, 0:2], target.at[u, chip], (send.at[way, u], recv.at[way, u]), device)
+
+        pltpu.make_async_copy(source.at[u, chip, 0:2], target.at[u, chip], stay.at[way, u]).start()
 
     def gathered(way, u, target):
         wait_for(target.at[u, chip], stay.at[way, u])
@@ -202,15 +197,8 @@
                     pair = [ref[pl.ds(row, UNIT, B), :] for ref in (ys, zs)]
                     blocks_out.append(jnp.concatenate(pair, axis=0).astype(BF16))
 
-                @pl.when(core == ic)
-                def _():
-                    for i in range(16):
-                        leaving[u, 4 * i + iz, ic] = blocks_out[i]
-
-                @pl.when(core != ic)
-                def _():
-                    for i in range(16):
-                        staged[u, 4 * i + iz] = blocks_out[i]
+                for i in range(16):
+                    leaving[u, 4 * i + iz, slot(ic)] = blocks_out[i]
 
         at = pl.multiple_of(u * UNIT, UNIT)
         filter_rows = gu[...].reshape(UNIT, lags)
@@ -233,7 +221,7 @@
             )
 
     def hand_out(u):
-        remote(staged.at[u], leaving.at[u, :, core], (hand_send.at[1, u], hand_recv.at[1, u]), mate)
+        remote(leaving.at[u, :, 2], leaving.at[u, :, core], (hand_send.at[1, u], hand_recv.at[1, u]), mate)
 
     def send_out(u):
         wait_for(leaving.at[u, :, 1 - core], hand_recv.at[1, u])
@@ -320,8 +308,8 @@
         some = h_ref.at[0:7, rows]
         for sem in (g_send, g_recv):
             wait_for(some, sem.at[u])
-        wait_for(staged.at[u], hand_send.at[0, u])
-        wait_for(staged.at[u], hand_send.at[1, u])
+        wait_for(going.at[u, :, 2], hand_send.at[0, u])
+        wait_for(leaving.at[u, :, 2], hand_send.at[1, u])
         wait_for(come.at[u, 0 : CHIPS - 1], send.at[0, u])
         wait_for(come.at[u, 0 : CHIPS - 1], send.at[1, u])
 
@@ -343,11 +331,9 @@
         scratch_shapes=[
             *[pltpu.VMEM(q.shape, BF16)] * 4,
             pltpu.VMEM(filter_taps.shape, F32),
+            pltpu.VMEM((UNITS, CHIPS, 3, BLOCK, B), BF16),
             pltpu.VMEM((UNITS, CHIPS, 2, BLOCK, B), BF16),
-            pltpu.VMEM((UNITS, CHIPS, BLOCK, B), BF16),
-            pltpu.VMEM((UNITS, CHIPS, 2, BLOCK, B), BF16),
-            pltpu.VMEM((UNITS, CHIPS, BLOCK, B), BF16),
-            pltpu.VMEM((UNITS, CHIPS, 2, BLOCK, B), BF16),
+            pltpu.VMEM((UNITS, CHIPS, 3, BLOCK, B), BF16),
             pltpu.VMEM((8, share, lags // 8), F32),
             pltpu.VMEM((share, 1, lags), F32),
             pltpu.VMEM((UNIT * PADDED, B), F32),

time: 78.1 us -> 75.2 us (0.963)
  Pallas kernels: 77.4 us -> 74.4 us
    pallas_call x1, Pallas kernels: 73 us -> 70 us  [exchange(): pl.pallas_call(exchange_kernel, in_specs=[anywhere] * 5 + [pl.BlockSpec(m...]
where the time goes in v5:
time: 75.2 us; the launch traced here: 75 us
  Pallas kernels  74.4 us (99%)
    pallas_call x1, Pallas kernels, exchange(): pl.pallas_call(exchange_kernel, in_specs=[anywhere] * 5 + [pl.BlockSpec(m...  70 us
    pallas_call x1, Pallas kernels, finish(): pl.pallas_call(finish_kernel, grid=(width // step,), in_specs=[pl.BlockSp...  4.4 us

profile of v5, /device:TPU:1, one launch (start us, length us, event | category | flops | bytes accessed | tf_op | source)
XLA Modules:
  0.0 75.0 jit_solution(11307151175943698547)
XLA Ops:
  0.6 70.0 %exchange.1 = (bf16[4,64,2,16,128]{4,3,2,1,0:T(8,128)(2,1)}, f32[8,32,256]{2,1,0:T(8,128)}, f32[32,128]{1,0:T(8,128)}) custom-call(bf16[128,4096]{1,0:T(8,128)(2,1)} %bitcast.17, bf16[128,4096]{1,0:T(8,128)(2,1)} %bitcast.10, bf16[128,4096]{1,0:T(8,128)(2,1)} %bitcast.12, bf16[128,4096]{1,0:T(8,128)(2,1)} %bitcast.14, f32[2048,256]{1,0:T(8,128)} %f_any.1, ...), custom_call_target="tpu_custom_call" | custom-call | tf_op jit(solution)/shard_map/exchange/pallas_call | solution.py:322
  70.6 4.4 %finish.1 = (bf16[128,4096]{1,0:T(8,128)(2,1)}, bf16[128,4096]{1,0:T(8,128)(2,1)}, bf16[128,4096]{1,0:T(8,128)(2,1)}, f32[256,256]{1,0:T(8,128)}, f32[1,32]{1,0:T(1,128)}) custom-call(bf16[4,4,4,4,2,16,128]{6,5,4,3,2,1,0:T(8,128)(2,1)} %bitcast.16, bf16[128,4096]{1,0:T(8,128)(2,1)} %bitcast.11, bf16[128,4096]{1,0:T(8,128)(2,1)} %bitcast.13, ...), custom_call_target="tpu_custom_call" | custom-call | tf_op jit(solution)/shard_map/finish/pallas_call | solution.py:402
